TPU v7x, 32 devices: a whole 2x2x4 slice. The times are simulated.
32 devices in a mesh: corr: 4 (over y, x), tile: 8 (over z, core).
Axes of the slice: x: 2, y: 2, z: 4, core: 2. Of those that a mesh axis runs over, the one named last changes fastest.
Arguments:
- visibilities: bfloat16 [2048, 8, 256], P(('corr', 'tile')), may hold values from -6 to 6
- coords: float32 [2048, 3, 256], P(('corr', 'tile')), may hold values from -12 to 12
- stations: int32 [2048, 2], P(('corr', 'tile')), may hold values from 0 to 511
- tile_ids: int32 [2048, 1], P(('corr', 'tile')), may hold values from 0 to 63; in each aligned block of 64 rows (0 to 63, 64 to 127, ...) at most 2 rows name the same one
- offsets: int32 [2048, 2], P(('corr', 'tile')), may hold values from 0 to 96
- screens: bfloat16 [512, 8, 1024], P('tile'), may hold values from -4 to 4
Outputs:
- grid_tiles: float32 [4, 64, 2, 128, 128], P('corr', 'tile')
Inputs may be any that keep to these rules, and one draw needn't show every extreme that they name: `tile_ids`: within the rows of one device (aligned blocks of 64 rows) no uv-tile is named more than 2 times, and some uv-tile exactly 2 times.
All inputs are finite; a program needn't handle non-finite values.
Results may differ from a plain program's by a relative error of at most 0.0061.
Values may be sent and summed in bfloat16 or wider, within the bound.
No kernel may reach another device: no remote copies, remote signals or barrier semaphores. Data moves between devices by JAX's collectives and lax.ppermute only.
A program may use at most 64 MiB of HBM per device.

v0:
```python
import functools
import math

import jax
import jax.numpy as jnp
import numpy as np
from jax import lax
from jax.experimental import pallas as pl
from jax.experimental.pallas import tpu as pltpu
from jax.sharding import PartitionSpec as P

SUB = 32
NT = 64
TILE_SIDE = 128
PIX = SUB * SUB
LANES = 128
VMEM_LIMIT = 36 * 1024 * 1024
VMEM_ALL = 63 * 1024 * 1024 + 512 * 1024

ROOT2 = math.sqrt(2.0)


def half_turn_series():
    grid = np.cos(np.pi * (np.arange(400) + 0.5) / 800.0) * 0.5
    z = grid * grid
    sine = np.polynomial.polynomial.Polynomial.fit(z, np.sin(np.pi * grid) / grid, 4, domain=[0, 0.25], window=[0, 0.25]).coef
    cosine = np.polynomial.polynomial.Polynomial.fit(z, np.cos(np.pi * grid), 4, domain=[0, 0.25], window=[0, 0.25]).coef
    return [float(x) * ROOT2 for x in sine], [float(x) * ROOT2 for x in cosine]


SINE, COSINE = half_turn_series()


def horner(coefficients, z):
    total = coefficients[-1]
    for value in coefficients[-2::-1]:
        total = total * z + value
    return total


def cis_turns(turns):
    t = turns - jnp.round(turns)
    z = t * t
    s = t * horner(SINE, z)
    c = horner(COSINE, z)
    return 1.0 - s * s, s * c


def image_kernel(ncorr, groups, vis_ref, coord_ref, *refs):
    out_refs, square = refs[:-1], refs[-1]
    me = lax.axis_index("corr")
    step = vis_ref.shape[0]
    nvis = vis_ref.shape[2]
    centred = (lax.broadcasted_iota(jnp.int32, (SUB, nvis), 0) - SUB // 2).astype(jnp.float32) * (1.0 / SUB)
    bend = 0.5 * centred * centred
    rows = ncorr * SUB

    def one(s):
        u = coord_ref[0, pl.ds(s, 1), :]
        v = coord_ref[1, pl.ds(s, 1), :]
        w = coord_ref[2, pl.ds(s, 1), :]
        sag = w * bend
        e_re, e_im = cis_turns(u * centred - sag)
        f_re, f_im = cis_turns(v * centred - sag)
        vis = vis_ref[s].astype(jnp.float32)
        g_re = []
        g_im = []
        for e in range(ncorr):
            vr = vis[e : e + 1]
            vi = vis[ncorr + e : ncorr + e + 1]
            g_re.append((vr * e_re - vi * e_im).astype(jnp.bfloat16))
            g_im.append((vr * e_im + vi * e_re).astype(jnp.bfloat16))
        left = jnp.concatenate([jnp.concatenate(g_re, axis=0), jnp.concatenate(g_im, axis=0)], axis=1)
        f_re = f_re.astype(jnp.bfloat16)
        f_im = f_im.astype(jnp.bfloat16)
        right = jnp.concatenate(
            [jnp.concatenate([f_re, f_im], axis=0), jnp.concatenate([-f_im, f_re], axis=0)], axis=1
        )
        image = lax.dot_general(left, right, (((1,), (1,)), ((), ())), preferred_element_type=jnp.float32)
        square[pl.ds(pl.multiple_of(s * rows, rows), rows), 0 : 2 * SUB] = image

    def several(i, carry):
        for j in range(4):
            one(i * 4 + j)
        return carry

    lax.fori_loop(0, step // 4, several, 0)

    lane = lax.broadcasted_iota(jnp.int32, (step, LANES), 1)
    per_tile = LANES // SUB
    halves = SUB // groups // per_tile
    for d in range(groups):
        first = (me ^ d) * (halves * per_tile)
        for h in range(halves):
            for e in range(ncorr):
                real = None
                imag = None
                for j in range(per_tile):
                    piece = square[pl.ds(first + (e * SUB + h * per_tile + j), step, stride=rows), :]
                    a = piece if j == 0 else pltpu.roll(piece, SUB * j, 1)
                    b = piece if j == 1 else pltpu.roll(piece, (SUB * (j - 1)) % LANES, 1)
                    keep = lane < SUB * (j + 1)
                    real = a if real is None else jnp.where(lane < SUB * j, real, a)
                    imag = b if imag is None else jnp.where(lane < SUB * j, imag, b)
                base = h * 2 * ncorr * LANES
                out_refs[d][:, base + e * LANES : base + (e + 1) * LANES] = real.astype(jnp.bfloat16)
                out_refs[d][:, base + (ncorr + e) * LANES : base + (ncorr + e + 1) * LANES] = imag.astype(jnp.bfloat16)


def make_images(visibilities, coords, groups):
    count, fields, nvis = visibilities.shape
    ncorr = fields // 2
    step = 16
    width = fields * PIX // groups
    return pl.pallas_call(
        functools.partial(image_kernel, ncorr, groups),
        grid=(count // step,),
        in_specs=[
            pl.BlockSpec((step, fields, nvis), lambda i: (i, 0, 0)),
            pl.BlockSpec((3, step, nvis), lambda i: (0, i, 0)),
        ],
        out_specs=[pl.BlockSpec((step, width), lambda i: (i, 0))] * groups,
        out_shape=[jax.ShapeDtypeStruct((count, width), jnp.bfloat16)] * groups,
        scratch_shapes=[pltpu.VMEM((step * ncorr * SUB, LANES), jnp.float32)],
        compiler_params=pltpu.CompilerParams(vmem_limit_bytes=VMEM_ALL),
        cost_estimate=pl.CostEstimate(flops=count << 27, bytes_accessed=2 << 20, transcendentals=0),
        name="images",
    )(visibilities, jnp.transpose(coords, (1, 0, 2)))


def plan_kernel(groups, owners, per_owner, count, every_ref, pick_ref, order_ref, place_ref, most_ref):
    nst = pick_ref.shape[1]
    n = groups * count
    together = LANES // count
    me = lax.axis_index("tile")
    lane = lax.broadcasted_iota(jnp.int32, (8, LANES), 1)
    number = lax.broadcasted_iota(jnp.int32, (count, nst), 1).astype(jnp.float32)
    before = lax.broadcasted_iota(jnp.int32, (n, n), 0) < lax.broadcasted_iota(jnp.int32, (n, n), 1)
    before = before.astype(jnp.float32).astype(jnp.bfloat16)
    owner_row = lax.broadcasted_iota(jnp.int32, (owners, n), 0).astype(jnp.float32)
    slot = lax.broadcasted_iota(jnp.int32, (LANES, n), 0).astype(jnp.float32)
    row = lax.broadcasted_iota(jnp.int32, (8, LANES), 0)

    def group(t):
        tiles = []
        for g in range(0, groups, together):
            joined = None
            for k in range(together):
                facts = every_ref[(g + k) * owners + t].astype(jnp.float32)
                facts = facts if k == 0 else pltpu.roll(facts, k * count, 1)
                joined = facts if k == 0 else jnp.where(lane < k * count, joined, facts)
            tiles.append(joined)
        return jnp.concatenate(tiles, axis=1)

    def ranks(facts):
        owner = jnp.floor(facts[0:1] * (1.0 / per_owner))
        hot = (owner_row == owner).astype(jnp.float32)
        ahead = jnp.dot(hot.astype(jnp.bfloat16), before, preferred_element_type=jnp.float32)
        return owner, jnp.sum(hot * ahead, axis=0, keepdims=True), jnp.sum(hot, axis=1, keepdims=True)

    for g in range(groups):
        columns = jnp.transpose(every_ref[g * owners + me].astype(jnp.float32))
        for which in range(2):
            at = which * n + g * count
            station = columns[:count, 3 + which : 4 + which]
            pick_ref[at : at + count, :] = (number == station).astype(jnp.float32).astype(jnp.bfloat16)
    owner, rank, held = ranks(group(me))
    order_ref[0:1, :] = owner
    order_ref[1:2, :] = rank

    most = jnp.zeros((owners, 1), jnp.float32)
    for t in range(owners):
        facts = group(t)
        owner, rank, held = ranks(facts)
        most = jnp.maximum(most, held)
        here = jnp.where(owner == me.astype(jnp.float32), 1.0, 0.0)
        hit = jnp.where(slot == jnp.where(here > 0.0, rank, -1.0), 1.0, 0.0).astype(jnp.bfloat16)
        local = facts[0:1] - owner * per_owner
        values = jnp.concatenate([facts[1:3], local, jnp.zeros((5, n), jnp.float32)], axis=0).astype(jnp.bfloat16)
        found = lax.dot_general(values, hit, (((1,), (1,)), ((), ())), preferred_element_type=jnp.float32)
        total = jnp.sum(here, axis=1, keepdims=True)
        place_ref[t] = jnp.where(row == 4, total, found).astype(jnp.int32)
    most_ref[...] = jnp.broadcast_to(jnp.max(most, axis=0, keepdims=True), most_ref.shape).astype(jnp.int32)


def make_plan(every, groups, owners, per_owner, count, nst):
    n = groups * count
    return pl.pallas_call(
        functools.partial(plan_kernel, groups, owners, per_owner, count),
        out_shape=[
            jax.ShapeDtypeStruct((2 * n, nst), jnp.bfloat16),
            jax.ShapeDtypeStruct((8, n), jnp.float32),
            jax.ShapeDtypeStruct((owners, 8, LANES), jnp.int32),
            jax.ShapeDtypeStruct((8, LANES), jnp.int32),
        ],
        compiler_params=pltpu.CompilerParams(vmem_limit_bytes=VMEM_LIMIT),
        cost_estimate=pl.CostEstimate(flops=1 << 30, bytes_accessed=1 << 20, transcendentals=0),
        name="plan",
    )(every)


def aterm_kernel(ncorr, owners, rows_of, *refs):
    groups = len(refs) - 7
    image_refs, refs = refs[:groups], refs[groups:]
    taper_ref, screen_ref, pick_ref, order_ref, out_ref, block_ref, jones_ref = refs
    count = image_refs[0].shape[0]
    n = groups * count
    me = lax.axis_index("corr")
    jones_ref[...] = jnp.dot(pick_ref[...], screen_ref[...], preferred_element_type=jnp.float32)
    taper = taper_ref[0]
    chunk = 16

    def part(ref, rows, field):
        return ref[rows, field * LANES : (field + 1) * LANES].astype(jnp.float32)

    def body(d, i, carry):
        held = pl.ds(pl.multiple_of(i * chunk, chunk), chunk)
        at = (me ^ d) * count + i * chunk
        rows = pl.ds(pl.multiple_of(at, chunk), chunk)
        far_rows = pl.ds(pl.multiple_of(at + n, chunk), chunk)
        image_re = [part(image_refs[d], held, e) for e in range(ncorr)]
        image_im = [part(image_refs[d], held, ncorr + e) for e in range(ncorr)]
        for row_out in range(2):
            mid_re = []
            mid_im = []
            for inner in range(2):
                m_re = 0.0
                m_im = 0.0
                for first in range(2):
                    near_re = part(jones_ref, rows, 2 * first + row_out)
                    near_im = part(jones_ref, rows, ncorr + 2 * first + row_out)
                    vis_re = image_re[2 * first + inner]
                    vis_im = image_im[2 * first + inner]
                    m_re = m_re + near_re * vis_re + near_im * vis_im
                    m_im = m_im + near_re * vis_im - near_im * vis_re
                mid_re.append(m_re)
                mid_im.append(m_im)
            for col_out in range(2):
                t_re = 0.0
                t_im = 0.0
                for inner in range(2):
                    far_re = part(jones_ref, far_rows, 2 * inner + col_out)
                    far_im = part(jones_ref, far_rows, ncorr + 2 * inner + col_out)
                    t_re = t_re + mid_re[inner] * far_re - mid_im[inner] * far_im
                    t_im = t_im + mid_re[inner] * far_im + mid_im[inner] * far_re
                place = 2 * (2 * row_out + col_out) * LANES
                block_ref[rows, place : place + LANES] = (t_re * taper).astype(jnp.bfloat16)
                block_ref[rows, place + LANES : place + 2 * LANES] = (t_im * taper).astype(jnp.bfloat16)
        return carry

    for d in range(groups):
        lax.fori_loop(0, count // chunk, functools.partial(body, d), 0)
    target = order_ref[0:1, :] * float(rows_of) + order_ref[1:2, :]
    row = lax.broadcasted_iota(jnp.int32, (owners * rows_of, n), 0).astype(jnp.float32)
    move = (row == target).astype(jnp.float32).astype(jnp.bfloat16)
    for e in range(ncorr):
        block = block_ref[:, 2 * e * LANES : 2 * (e + 1) * LANES]
        out_ref[e] = jnp.dot(move, block, preferred_element_type=jnp.float32).astype(jnp.bfloat16)


def apply_aterms(images, screens, pick, order, taper, ncorr, owners, rows):
    count = images[0].shape[0]
    n = count * len(images)
    nst = screens.shape[0]
    half = 2 * ncorr * LANES
    halves = screens.shape[1] // half
    return pl.pallas_call(
        functools.partial(aterm_kernel, ncorr, owners, rows),
        grid=(halves,),
        in_specs=[pl.BlockSpec((count, half), lambda h: (0, h))] * len(images)
        + [
            pl.BlockSpec((1, 1, LANES), lambda h: (h, 0, 0)),
            pl.BlockSpec((nst, half), lambda h: (0, h)),
            pl.BlockSpec(pick.shape, lambda h: (0, 0)),
            pl.BlockSpec(order.shape, lambda h: (0, 0)),
        ],
        out_specs=pl.BlockSpec((ncorr, owners * rows, 2 * LANES), lambda h: (0, 0, h)),
        out_shape=jax.ShapeDtypeStruct((ncorr, owners * rows, halves * 2 * LANES), jnp.bfloat16),
        scratch_shapes=[pltpu.VMEM((n, half), jnp.bfloat16), pltpu.VMEM((2 * n, half), jnp.float32)],
        compiler_params=pltpu.CompilerParams(vmem_limit_bytes=VMEM_ALL),
        cost_estimate=pl.CostEstimate(flops=6 << 30, bytes_accessed=8 << 20, transcendentals=0),
        name="aterms",
    )(*images, taper, screens, pick, order)


def grid_kernel(rows, place_ref, block_ref, col_ref, row_ref, out_ref, half_ref, uv_ref, turned_a, turned_b, re_a, im_a, re_b, im_b):
    groups, total, depth = block_ref.shape
    sources = total // rows
    per_slot = 2 * PIX // LANES
    quarters = depth // LANES
    for g in range(groups):
        half_ref[g] = jnp.dot(block_ref[g], col_ref[...], preferred_element_type=jnp.float32).astype(jnp.bfloat16)
    for q in range(quarters):
        left = jnp.concatenate([half_ref[g, :, q * LANES : (q + 1) * LANES] for g in range(groups)], axis=1)
        uv = jnp.dot(left, row_ref[...], preferred_element_type=jnp.float32)
        for part in range(2):
            for i in range(2):
                j = part * 2 + i
                uv_ref[pl.ds(part * 8 + 2 * q + i, total, stride=per_slot), :] = uv[:, j * LANES : (j + 1) * LANES]
    for ref in (re_a, im_a, re_b, im_b):
        ref[...] = jnp.zeros_like(ref)

    lane = lax.broadcasted_iota(jnp.int32, (8, LANES), 1)
    pieces = LANES // SUB
    tall = 2 * pieces * 8
    batch = 8
    longest = place_ref[0, 4, 0]
    for t in range(1, sources):
        longest = jnp.maximum(longest, place_ref[t, 4, 0])
    trips = (longest + (batch - 1)) // batch
    turned = (turned_a, turned_b)

    def turn(t, i):
        for b in range(batch):
            j = i * batch + b
            y = place_ref[t, 1, j]
            inside = (lane >= y) & (lane < y + SUB)
            for part in range(2):
                at = pl.multiple_of((t * rows + j) * per_slot + part * 8, 8)
                block = uv_ref[pl.ds(at, 8), :]
                for g in range(pieces):
                    moved = pltpu.roll(block, (y + (LANES - g * SUB)) & (LANES - 1), 1)
                    at = pl.multiple_of(j * tall + (part * pieces + g) * 8, 8)
                    turned[t % 2][pl.ds(at, 8), :] = jnp.where(inside, moved, 0.0)

    def add(t, i):
        for b in range(batch):
            j = i * batch + b
            row = place_ref[t, 2, j] * TILE_SIDE + place_ref[t, 0, j]
            for part, ref in enumerate((re_a, im_a) if b % 2 == 0 else (re_b, im_b)):
                at = pl.multiple_of(j * tall + part * pieces * 8, 8)
                ref[pl.ds(row, SUB), :] = ref[pl.ds(row, SUB), :] + turned[t % 2][pl.ds(at, SUB), :]

    for t in range(sources + 1):

        def both(i, carry):
            if t < sources:
                turn(t, i)
            if t > 0:
                add(t - 1, i)
            return carry

        lax.fori_loop(0, trips, both, 0)

    for k in range(out_ref.shape[0]):
        span = slice(k * TILE_SIDE, (k + 1) * TILE_SIDE)
        for part, (one, two) in enumerate(((re_a, re_b), (im_a, im_b))):
            out_ref[k, part] = one[span, :] + two[span, :]


def place_on_grid(places, blocks, rows, tables, per_owner):
    groups, total, depth = blocks.shape
    whole = pl.BlockSpec(memory_space=pltpu.VMEM)
    accumulator = pltpu.VMEM((per_owner * TILE_SIDE, TILE_SIDE), jnp.float32)
    return pl.pallas_call(
        functools.partial(grid_kernel, rows),
        in_specs=[pl.BlockSpec(memory_space=pltpu.SMEM), whole, whole, whole],
        out_specs=whole,
        out_shape=jax.ShapeDtypeStruct((per_owner, 2, TILE_SIDE, TILE_SIDE), jnp.float32),
        scratch_shapes=[
            pltpu.VMEM((groups, total, depth), jnp.bfloat16),
            pltpu.VMEM((total * 2 * PIX // LANES, LANES), jnp.float32),
            pltpu.VMEM((rows * 2 * PIX // SUB, LANES), jnp.float32),
            pltpu.VMEM((rows * 2 * PIX // SUB, LANES), jnp.float32),
            accumulator,
            accumulator,
            accumulator,
            accumulator,
        ],
        compiler_params=pltpu.CompilerParams(vmem_limit_bytes=VMEM_LIMIT),
        name="grid",
    )(places, blocks, *tables)


def uv_tables(groups):
    quad = LANES // SUB
    halves = SUB // (groups * quad)
    index = np.arange(SUB) - SUB // 2
    factor = np.exp(-2j * np.pi / SUB * ((index[:, None] * index[None, :]) % SUB))

    def parts(table, axis):
        upper = np.stack([table.real, table.imag], axis=axis)
        lower = np.stack([-table.imag, table.real], axis=axis)
        return upper, lower

    col = (factor / SUB).reshape(SUB, 4, 4, 2).transpose(2, 0, 3, 1)
    first = np.zeros((halves, 2, quad, SUB, 4, halves, 2, quad, 2, 4))
    for p, table in enumerate(parts(col, 0)):
        for h in range(halves):
            for r in range(quad):
                first[h, p, r, :, :, h, :, r] = table.transpose(2, 1, 0, 3, 4)
    second = np.zeros((groups, halves, 2, quad, 2, 4, 2, 2, 4, SUB))
    row = factor.reshape(groups, halves, quad, SUB)
    for p, table in enumerate(parts(row, 0)):
        for i in range(2):
            for g in range(4):
                second[:, :, p, :, i, g, :, i, g, :] = table.transpose(1, 2, 3, 0, 4)
    size = halves * 2 * LANES
    first = first.reshape(size, 4 * halves * 2 * quad * 8)
    second = second.reshape(groups * halves * 2 * quad * 8, 4 * LANES)
    return first.astype(jnp.bfloat16), second.astype(jnp.bfloat16)


def taper_table(scale):
    pos = (np.arange(SUB) - SUB / 2 + 0.5) / (SUB / 2)
    one = 1.0 - 0.8 * pos * pos
    return (one[:, None] * one[None, :] * scale).astype(np.float32)


def per_device(visibilities, coords, stations, tile_ids, offsets, screens):
    count, fields, nvis = visibilities.shape
    ncorr = fields // 2
    groups = lax.axis_size("corr")
    owners = lax.axis_size("tile")
    corr = lax.axis_index("corr")
    tile = lax.axis_index("tile")
    per_owner = NT // owners
    full = per_owner * groups * (2 * count // NT)
    halves = PIX // (groups * LANES)
    local = PIX // groups

    part = lax.dynamic_slice_in_dim(screens, corr * local, local, axis=2)
    part = part.reshape(-1, fields, halves, LANES).transpose(0, 2, 1, 3).reshape(-1, fields * local)
    all_screens = lax.all_gather(part, "tile", axis=0, tiled=True)

    images = list(make_images(visibilities, coords, groups))
    tile_ids, offsets, stations, images[0] = lax.optimization_barrier((tile_ids, offsets, stations, images[0]))
    facts = jnp.concatenate([tile_ids.T, offsets.T, stations.T], axis=0)
    facts = jnp.pad(facts, ((0, 8 - facts.shape[0]), (0, LANES - count)))
    every = jnp.broadcast_to(facts[None], (groups * owners, 8, LANES))
    every = lax.all_to_all(every, ("corr", "tile"), split_axis=0, concat_axis=0, tiled=True)

    images = [
        lax.ppermute(piece, "corr", [(i, i ^ d) for i in range(groups)]) if d else piece for d, piece in enumerate(images)
    ]
    pick, order, places, most = make_plan(every, groups, owners, per_owner, count, all_screens.shape[0])

    taper = jnp.asarray(taper_table(1.0 / nvis)).reshape(groups, halves, 1, LANES)
    taper = lax.dynamic_index_in_dim(taper, corr, axis=0, keepdims=False)
    tables = tuple(jnp.asarray(table) for table in uv_tables(groups))

    def finish(rows, images, screens, pick, order, places, taper):
        sending = apply_aterms(images, screens, pick, order, taper, ncorr, owners, rows)
        received = lax.all_to_all(
            sending.reshape(groups * owners, rows, 2 * local), ("corr", "tile"), split_axis=0, concat_axis=0, tiled=True
        )
        return place_on_grid(places, received.reshape(groups, owners * rows, 2 * local), rows, tables, per_owner)

    heights = sorted({min(full, -(-full * share // 64) * 8) for share in (5, 6, 8)})
    branches = [functools.partial(finish, rows) for rows in heights]
    if len(heights) == 1:
        grid = branches[0](images, all_screens, pick, order, places, taper)
    else:
        index = sum((most[0, 0] > rows).astype(jnp.int32) for rows in heights[:-1])
        grid = lax.switch(index, branches, images, all_screens, pick, order, places, taper)
    return grid[None]


def solution(mesh):
    return jax.shard_map(
        per_device,
        mesh=mesh,
        in_specs=(
            P(("corr", "tile"), None, None),
            P(("corr", "tile"), None, None),
            P(("corr", "tile"), None),
            P(("corr", "tile"), None),
            P(("corr", "tile"), None),
            P("tile", None, None),
        ),
        out_specs=P("corr", "tile", None, None, None),
        check_vma=False,
    )
```

profile of v0, /device:TPU:0, one launch (start us, length us, event | category | flops | bytes accessed | tf_op | source)
XLA Modules:
  0.0 106.5 jit_solution(11346696610911666660)
XLA Ops:
  6.5 1.0 constant_dynamic-slice_fusion.3
  7.5 0.8 copy.18
  8.3 0.0 all-gather.2.cloned.1.call-update
  8.3 0.0 copy-start.7
  8.3 0.0 copy-start.8
  8.3 0.0 copy-start.9
  8.3 12.6 %images.1 = (bf16[64,2048]{1,0:T(8,128)(2,1)}, bf16[64,2048]{1,0:T(8,128)(2,1)}, bf16[64,2048]{1,0:T(8,128)(2,1)}, bf16[64,2048]{1,0:T(8,128)(2,1)}) custom-call(bf16[64,8,256]{2,1,0:T(8,128)(2,1)} %vis_ref.1, f32[3,64,256]{2,1,0:T(8,128)} %bitcast.45), custom_call_target="tpu_custom_call" | custom-call | flops 8589934592 | bytes 2097152 | tf_op jit(solution)/shard_map/images/pallas_call | solution.py:115
  21.0 0.7 broadcast_in_dim.16
  21.6 7.3 %all-to-all-start.3 = ((s32[32,8,128]{2,1,0:T(8,128)}), s32[32,8,128]{2,1,0:T(8,128)S(1)}, u32[]{:S(2)}, u32[]{:S(2)}) async-start(s32[32,8,128]{2,1,0:T(8,128)} %broadcast_in_dim.16), calls=%async_computation.3 | async-start | bytes 262144 | tf_op jit(solution)/shard_map/all_to_all | solution.py:431
  28.9 1.8 %collective-permute-start = (bf16[64,2048]{1,0:T(8,128)(2,1)}, bf16[64,2048]{1,0:T(8,128)(2,1)S(1)}, u32[]{:S(2)}, u32[]{:S(2)}) collective-permute-start(bf16[64,2048]{1,0:T(8,128)(2,1)} %get-tuple-element.169), channel_id=1, source_target_pairs={{0,8},{8,0},{16,24},{24,16},{1,9},{9,1},{17,25},{25,17},{2,10},{10... | collective-permute-start | bytes 786440 | tf_op jit(solution)/shard_map/ppermute | solution.py:434
  30.8 1.5 %collective-permute-start.1 = (bf16[64,2048]{1,0:T(8,128)(2,1)}, bf16[64,2048]{1,0:T(8,128)(2,1)}, u32[]{:S(2)}, u32[]{:S(2)}) collective-permute-start(bf16[64,2048]{1,0:T(8,128)(2,1)} %get-tuple-element.170), channel_id=1, source_target_pairs={{0,16},{8,24},{16,0},{24,8},{1,17},{9,25},{17,1},{25,9},{2,18},{10... | collective-permute-start | bytes 786440 | tf_op jit(solution)/shard_map/ppermute | solution.py:434
  32.2 0.3 collective-permute-start.2
  32.5 7.8 %all-to-all-done.3.every_ref = s32[32,8,128]{2,1,0:T(8,128)S(1)} async-done(((s32[32,8,128]{2,1,0:T(8,128)}), s32[32,8,128]{2,1,0:T(8,128)S(1)}, u32[]{:S(2)}, u32[]{:S(2)}) %all-to-all-start.3) | async-done | bytes 131104 | tf_op jit(solution)/shard_map/all_to_all | solution.py:431
  40.3 1.1 %plan.1 = (bf16[512,512]{1,0:T(8,128)(2,1)}, f32[8,256]{1,0:T(8,128)S(1)}, s32[8,8,128]{2,1,0:T(8,128)S(1)}, s32[8,128]{1,0:T(8,128)S(1)}) custom-call(s32[32,8,128]{2,1,0:T(8,128)S(1)} %all-to-all-done.3.every_ref), custom_call_target="tpu_custom_call" | custom-call | flops 1073741824 | bytes 1048576 | tf_op jit(solution)/shard_map/plan/pallas_call | solution.py:188
  41.4 0.5 slice.4
  43.1 0.0 collective-permute-done
  43.1 2.8 %collective-permute-done.1 = bf16[64,2048]{1,0:T(8,128)(2,1)} collective-permute-done((bf16[64,2048]{1,0:T(8,128)(2,1)}, bf16[64,2048]{1,0:T(8,128)(2,1)}, u32[]{:S(2)}, u32[]{:S(2)}) %collective-permute-start.1) | collective-permute-done | bytes 262176 | tf_op jit(solution)/shard_map/ppermute | solution.py:434
  45.8 0.0 collective-permute-done.2
  45.9 53.8 %conditional.1 = (f32[1,8,2,128,128]{4,3,2,1,0:T(8,128)}) conditional(s32[]{:T(128)} %bitcast.19, (f32[32,32]{1,0:T(8,128)S(1)}, s32[]{:T(128)}, bf16[64,2048]{1,0:T(8,128)(2,1)}, bf16[64,2048]{1,0:T(8,128)(2,1)S(1)}, bf16[64,2048]{1,0:T(8,128)(2,1)}, /*index=5*/bf16[64,2048]{1,0:T(8,128)(2,1)}, bf16[512,2048]{1,0:T(8,128)(2,1)}, ...), branch_computations={%region_0.1_spmd, %region_1.2_spmd, %region_2.3_spmd} | conditional | flops 6442450944 | bytes 16787558 | solution.py:455
  45.9 0.1 reshape.34
  46.0 0.6 constant_dynamic-slice_fusion
  46.5 5.9 %aterms.3 = bf16[4,320,512]{2,1,0:T(8,128)(2,1)} custom-call(bf16[64,2048]{1,0:T(8,128)(2,1)} %get-tuple-element.116.refs_0_, bf16[64,2048]{1,0:T(8,128)(2,1)S(1)} %get-tuple-element.117.refs_1_, bf16[64,2048]{1,0:T(8,128)(2,1)} %get-tuple-element.118.refs_2_, bf16[64,2048]{1,0:T(8,128)(2,1)} %get-tuple-element.119.refs_3_, f32[2,1,128]{2,1,0:T(1,128)} %bitcast.39, ...), custom_call_target="tpu_custom_call" | custom-call | flops 6442450944 | bytes 8388608 | tf_op jit(solution)/shard_map/cond/branch_0_fun/aterms/pallas_call | solution.py:267
  52.5 37.3 %all_to_all.17 = bf16[32,40,512]{2,1,0:T(8,128)(2,1)S(1)} all-to-all(bf16[32,40,512]{2,1,0:T(8,128)(2,1)} %bitcast.33), channel_id=1, replica_groups=mesh['corr'=4,'tile'=8] {'corr','tile'}, dimensions={0} | all-to-all | bytes 2621440 | tf_op jit(solution)/shard_map/cond/branch_0_fun/all_to_all | solution.py:444
  89.8 9.9 %grid.3 = f32[8,2,128,128]{3,2,1,0:T(8,128)} custom-call(s32[8,8,128]{2,1,0:T(8,128)S(1)} %get-tuple-element.115.place_ref, bf16[4,320,512]{2,1,0:T(8,128)(2,1)S(1)} %bitcast.30, bf16[512,512]{1,0:T(8,128)(2,1)S(1)} %copy-done.3, bf16[512,512]{1,0:T(8,128)(2,1)S(1)} %copy-done), custom_call_target="tpu_custom_call" | custom-call | tf_op jit(solution)/shard_map/cond/branch_0_fun/grid/pallas_call | solution.py:355
  (13 shorter events, 0.0 us)
Async XLA Ops:
  6.5 39.3 %all-gather.2.cloned.1.call-start = ((), (), s32[]{:S(2)}) async-start(), calls=%async_computation.4 | async-start | bytes 2359296 | tf_op jit(solution)/shard_map/all_gather | solution.py:424
  8.3 12.6 %copy-start.7 = (s32[64,2]{0,1:T(2,128)S(1)}, s32[64,2]{0,1:T(2,128)}, u32[]{:S(2)}) copy-start(s32[64,2]{0,1:T(2,128)} %param.14) | copy-start | bytes 1540
  8.3 12.6 %copy-start.8 = (s32[64,2]{0,1:T(2,128)S(1)}, s32[64,2]{0,1:T(2,128)}, u32[]{:S(2)}) copy-start(s32[64,2]{0,1:T(2,128)} %param.16) | copy-start | bytes 1540
  8.3 12.6 %copy-start.9 = (s32[64,1]{0,1:T(1,128)S(1)}, s32[64,1]{0,1:T(1,128)}, u32[]{:S(2)}) copy-start(s32[64,1]{0,1:T(1,128)} %param.15) | copy-start | bytes 772
  21.6 18.7 %all-to-all-start.3 = ((s32[32,8,128]{2,1,0:T(8,128)}), s32[32,8,128]{2,1,0:T(8,128)S(1)}, u32[]{:S(2)}, u32[]{:S(2)}) async-start(s32[32,8,128]{2,1,0:T(8,128)} %broadcast_in_dim.16), calls=%async_computation.3 | async-start | bytes 262144 | tf_op jit(solution)/shard_map/all_to_all | solution.py:431
  28.9 14.1 %collective-permute-start = (bf16[64,2048]{1,0:T(8,128)(2,1)}, bf16[64,2048]{1,0:T(8,128)(2,1)S(1)}, u32[]{:S(2)}, u32[]{:S(2)}) collective-permute-start(bf16[64,2048]{1,0:T(8,128)(2,1)} %get-tuple-element.169), channel_id=1, source_target_pairs={{0,8},{8,0},{16,24},{24,16},{1,9},{9,1},{17,25},{25,17},{2,10},{10... | collective-permute-start | bytes 786440 | tf_op jit(solution)/shard_map/ppermute | solution.py:434
  30.8 15.1 %collective-permute-start.1 = (bf16[64,2048]{1,0:T(8,128)(2,1)}, bf16[64,2048]{1,0:T(8,128)(2,1)}, u32[]{:S(2)}, u32[]{:S(2)}) collective-permute-start(bf16[64,2048]{1,0:T(8,128)(2,1)} %get-tuple-element.170), channel_id=1, source_target_pairs={{0,16},{8,24},{16,0},{24,8},{1,17},{9,25},{17,1},{25,9},{2,18},{10... | collective-permute-start | bytes 786440 | tf_op jit(solution)/shard_map/ppermute | solution.py:434
  32.2 13.6 %copy-start.6 = (f32[32,32]{1,0:T(8,128)S(1)}, f32[32,32]{1,0:T(8,128)}, u32[]{:S(2)}) copy-start(f32[32,32]{1,0:T(8,128)} %constant.47.clone) | copy-start | bytes 12292
  32.2 13.6 %collective-permute-start.2 = (bf16[64,2048]{1,0:T(8,128)(2,1)}, bf16[64,2048]{1,0:T(8,128)(2,1)}, u32[]{:S(2)}, u32[]{:S(2)}) collective-permute-start(bf16[64,2048]{1,0:T(8,128)(2,1)} %get-tuple-element.171), channel_id=1, source_target_pairs={{0,24},{8,16},{16,8},{24,0},{1,25},{9,17},{17,9},{25,1},{2,26},{10... | collective-permute-start | bytes 786440 | tf_op jit(solution)/shard_map/ppermute | solution.py:434
  52.5 37.3 %copy-start = (bf16[512,512]{1,0:T(8,128)(2,1)S(1)}, bf16[512,512]{1,0:T(8,128)(2,1)}, u32[]{:S(2)}) copy-start(bf16[512,512]{1,0:T(8,128)(2,1)} %get-tuple-element.126.row_ref) | copy-start | bytes 1572868 | tf_op jit(solution)/shard_map/cond
  52.5 37.3 %copy-start.3 = (bf16[512,512]{1,0:T(8,128)(2,1)S(1)}, bf16[512,512]{1,0:T(8,128)(2,1)}, u32[]{:S(2)}) copy-start(bf16[512,512]{1,0:T(8,128)(2,1)} %get-tuple-element.125.col_ref) | copy-start | bytes 1572868 | tf_op jit(solution)/shard_map/cond
Sparse Core Ops, SparseCore 0:
  9.0 35.1 all-gather.1
where the time goes:
time: 107 us
  blocking collectives  37.3 us (35%)
  Pallas kernels  29.5 us (28%)
  between operations  14.6 us (14%)
  starting transfers between devices  10.9 us (10%)
  waiting for transfers between devices  10.6 us (10%)
  local copies, waits for them, and re-layouts  3.59 us (3%)
    all_to_all x1, blocking collectives, finish(): lax.all_to_all(sending.reshape(groups * owners, rows, 2 * local), ('corr'...  37.3 us
    pallas_call x1, Pallas kernels, make_images(): pl.pallas_call(functools.partial(image_kernel, ncorr, groups), grid=(coun...  12.6 us
    pallas_call x1, Pallas kernels, place_on_grid(): pl.pallas_call(functools.partial(grid_kernel, rows), in_specs=[pl.BlockSp...  9.87 us
    all_to_all x1, waiting for transfers between devices, per_device(): lax.all_to_all(every, ('corr', 'tile'), split_axis=0, concat_axis=0, tile...  7.81 us
    all_to_all x1, starting transfers between devices, per_device(): lax.all_to_all(every, ('corr', 'tile'), split_axis=0, concat_axis=0, tile...  7.3 us
    pallas_call x1, Pallas kernels, apply_aterms(): pl.pallas_call(functools.partial(aterm_kernel, ncorr, owners, rows), grid...  5.95 us
    ppermute x3, starting transfers between devices, per_device(): lax.ppermute(piece, 'corr', [(i, i ^ d) for i in range(groups)])  3.55 us
    ppermute x3, waiting for transfers between devices, per_device(): lax.ppermute(piece, 'corr', [(i, i ^ d) for i in range(groups)])  2.78 us
  transfers between devices with their start and end apart: 5, of which 2 were waited for; matrix products, arithmetic and copies ran while one was open for 1% of the time, Pallas kernels for 13%

commit v1 on v0

--- a/solution.py
+++ b/solution.py
@@ -23,7 +23,7 @@
 def half_turn_series():
     grid = np.cos(np.pi * (np.arange(400) + 0.5) / 800.0) * 0.5
     z = grid * grid
-    sine = np.polynomial.polynomial.Polynomial.fit(z, np.sin(np.pi * grid) / grid, 4, domain=[0, 0.25], window=[0, 0.25]).coef
+    sine = np.polynomial.polynomial.Polynomial.fit(z, np.sin(np.pi * grid) / grid, 3, domain=[0, 0.25], window=[0, 0.25]).coef
     cosine = np.polynomial.polynomial.Polynomial.fit(z, np.cos(np.pi * grid), 4, domain=[0, 0.25], window=[0, 0.25]).coef
     return [float(x) * ROOT2 for x in sine], [float(x) * ROOT2 for x in cosine]
 
@@ -54,6 +54,7 @@
     centred = (lax.broadcasted_iota(jnp.int32, (SUB, nvis), 0) - SUB // 2).astype(jnp.float32) * (1.0 / SUB)
     bend = 0.5 * centred * centred
     rows = ncorr * SUB
+    pitch = rows + 1
 
     def one(s):
         u = coord_ref[0, pl.ds(s, 1), :]
@@ -77,7 +78,7 @@
             [jnp.concatenate([f_re, f_im], axis=0), jnp.concatenate([-f_im, f_re], axis=0)], axis=1
         )
         image = lax.dot_general(left, right, (((1,), (1,)), ((), ())), preferred_element_type=jnp.float32)
-        square[pl.ds(pl.multiple_of(s * rows, rows), rows), 0 : 2 * SUB] = image
+        square[pl.ds(s * pitch, rows), 0 : 2 * SUB] = image
 
     def several(i, carry):
         for j in range(4):
@@ -96,7 +97,7 @@
                 real = None
                 imag = None
                 for j in range(per_tile):
-                    piece = square[pl.ds(first + (e * SUB + h * per_tile + j), step, stride=rows), :]
+                    piece = square[pl.ds(first + (e * SUB + h * per_tile + j), step, stride=pitch), :]
                     a = piece if j == 0 else pltpu.roll(piece, SUB * j, 1)
                     b = piece if j == 1 else pltpu.roll(piece, (SUB * (j - 1)) % LANES, 1)
                     keep = lane < SUB * (j + 1)
@@ -121,7 +122,7 @@
         ],
         out_specs=[pl.BlockSpec((step, width), lambda i: (i, 0))] * groups,
         out_shape=[jax.ShapeDtypeStruct((count, width), jnp.bfloat16)] * groups,
-        scratch_shapes=[pltpu.VMEM((step * ncorr * SUB, LANES), jnp.float32)],
+        scratch_shapes=[pltpu.VMEM((step * (ncorr * SUB + 1), LANES), jnp.float32)],
         compiler_params=pltpu.CompilerParams(vmem_limit_bytes=VMEM_ALL),
         cost_estimate=pl.CostEstimate(flops=count << 27, bytes_accessed=2 << 20, transcendentals=0),
         name="images",
@@ -199,15 +200,18 @@
     )(every)
 
 
-def aterm_kernel(ncorr, owners, rows_of, *refs):
-    groups = len(refs) - 7
+def aterm_kernel(ncorr, owners, rows_of, scale, *refs):
+    groups = len(refs) - 6
     image_refs, refs = refs[:groups], refs[groups:]
-    taper_ref, screen_ref, pick_ref, order_ref, out_ref, block_ref, jones_ref = refs
+    screen_ref, pick_ref, order_ref, out_ref, block_ref, jones_ref = refs
     count = image_refs[0].shape[0]
     n = groups * count
     me = lax.axis_index("corr")
     jones_ref[...] = jnp.dot(pick_ref[...], screen_ref[...], preferred_element_type=jnp.float32)
-    taper = taper_ref[0]
+    pixel = lax.broadcasted_iota(jnp.int32, (1, LANES), 1) + (me * pl.num_programs(0) + pl.program_id(0)) * LANES
+    row_at = ((pixel // SUB).astype(jnp.float32) - (SUB - 1) / 2.0) * (2.0 / SUB)
+    col_at = ((pixel % SUB).astype(jnp.float32) - (SUB - 1) / 2.0) * (2.0 / SUB)
+    taper = (1.0 - 0.8 * row_at * row_at) * (1.0 - 0.8 * col_at * col_at) * scale
     chunk = 16
 
     def part(ref, rows, field):
@@ -258,18 +262,17 @@
         out_ref[e] = jnp.dot(move, block, preferred_element_type=jnp.float32).astype(jnp.bfloat16)
 
 
-def apply_aterms(images, screens, pick, order, taper, ncorr, owners, rows):
+def apply_aterms(images, screens, pick, order, scale, ncorr, owners, rows):
     count = images[0].shape[0]
     n = count * len(images)
     nst = screens.shape[0]
     half = 2 * ncorr * LANES
     halves = screens.shape[1] // half
     return pl.pallas_call(
-        functools.partial(aterm_kernel, ncorr, owners, rows),
+        functools.partial(aterm_kernel, ncorr, owners, rows, scale),
         grid=(halves,),
         in_specs=[pl.BlockSpec((count, half), lambda h: (0, h))] * len(images)
         + [
-            pl.BlockSpec((1, 1, LANES), lambda h: (h, 0, 0)),
             pl.BlockSpec((nst, half), lambda h: (0, h)),
             pl.BlockSpec(pick.shape, lambda h: (0, 0)),
             pl.BlockSpec(order.shape, lambda h: (0, 0)),
@@ -280,13 +283,13 @@
         compiler_params=pltpu.CompilerParams(vmem_limit_bytes=VMEM_ALL),
         cost_estimate=pl.CostEstimate(flops=6 << 30, bytes_accessed=8 << 20, transcendentals=0),
         name="aterms",
-    )(*images, taper, screens, pick, order)
+    )(*images, screens, pick, order)
 
 
 def grid_kernel(rows, place_ref, block_ref, col_ref, row_ref, out_ref, half_ref, uv_ref, turned_a, turned_b, re_a, im_a, re_b, im_b):
     groups, total, depth = block_ref.shape
     sources = total // rows
-    per_slot = 2 * PIX // LANES
+    per_slot = 2 * PIX // LANES + 1
     quarters = depth // LANES
     for g in range(groups):
         half_ref[g] = jnp.dot(block_ref[g], col_ref[...], preferred_element_type=jnp.float32).astype(jnp.bfloat16)
@@ -316,7 +319,7 @@
             y = place_ref[t, 1, j]
             inside = (lane >= y) & (lane < y + SUB)
             for part in range(2):
-                at = pl.multiple_of((t * rows + j) * per_slot + part * 8, 8)
+                at = (t * rows + j) * per_slot + part * 8
                 block = uv_ref[pl.ds(at, 8), :]
                 for g in range(pieces):
                     moved = pltpu.roll(block, (y + (LANES - g * SUB)) & (LANES - 1), 1)
@@ -359,7 +362,7 @@
         out_shape=jax.ShapeDtypeStruct((per_owner, 2, TILE_SIDE, TILE_SIDE), jnp.float32),
         scratch_shapes=[
             pltpu.VMEM((groups, total, depth), jnp.bfloat16),
-            pltpu.VMEM((total * 2 * PIX // LANES, LANES), jnp.float32),
+            pltpu.VMEM((total * (2 * PIX // LANES + 1), LANES), jnp.float32),
             pltpu.VMEM((rows * 2 * PIX // SUB, LANES), jnp.float32),
             pltpu.VMEM((rows * 2 * PIX // SUB, LANES), jnp.float32),
             accumulator,
@@ -401,12 +404,6 @@
     return first.astype(jnp.bfloat16), second.astype(jnp.bfloat16)
 
 
-def taper_table(scale):
-    pos = (np.arange(SUB) - SUB / 2 + 0.5) / (SUB / 2)
-    one = 1.0 - 0.8 * pos * pos
-    return (one[:, None] * one[None, :] * scale).astype(np.float32)
-
-
 def per_device(visibilities, coords, stations, tile_ids, offsets, screens):
     count, fields, nvis = visibilities.shape
     ncorr = fields // 2
@@ -423,24 +420,21 @@
     part = part.reshape(-1, fields, halves, LANES).transpose(0, 2, 1, 3).reshape(-1, fields * local)
     all_screens = lax.all_gather(part, "tile", axis=0, tiled=True)
 
-    images = list(make_images(visibilities, coords, groups))
-    tile_ids, offsets, stations, images[0] = lax.optimization_barrier((tile_ids, offsets, stations, images[0]))
     facts = jnp.concatenate([tile_ids.T, offsets.T, stations.T], axis=0)
     facts = jnp.pad(facts, ((0, 8 - facts.shape[0]), (0, LANES - count)))
     every = jnp.broadcast_to(facts[None], (groups * owners, 8, LANES))
     every = lax.all_to_all(every, ("corr", "tile"), split_axis=0, concat_axis=0, tiled=True)
 
+    images = make_images(visibilities, coords, groups)
     images = [
         lax.ppermute(piece, "corr", [(i, i ^ d) for i in range(groups)]) if d else piece for d, piece in enumerate(images)
     ]
     pick, order, places, most = make_plan(every, groups, owners, per_owner, count, all_screens.shape[0])
 
-    taper = jnp.asarray(taper_table(1.0 / nvis)).reshape(groups, halves, 1, LANES)
-    taper = lax.dynamic_index_in_dim(taper, corr, axis=0, keepdims=False)
     tables = tuple(jnp.asarray(table) for table in uv_tables(groups))
 
-    def finish(rows, images, screens, pick, order, places, taper):
-        sending = apply_aterms(images, screens, pick, order, taper, ncorr, owners, rows)
+    def finish(rows, images, screens, pick, order, places):
+        sending = apply_aterms(images, screens, pick, order, 1.0 / nvis, ncorr, owners, rows)
         received = lax.all_to_all(
             sending.reshape(groups * owners, rows, 2 * local), ("corr", "tile"), split_axis=0, concat_axis=0, tiled=True
         )
@@ -449,10 +443,10 @@
     heights = sorted({min(full, -(-full * share // 64) * 8) for share in (5, 6, 8)})
     branches = [functools.partial(finish, rows) for rows in heights]
     if len(heights) == 1:
-        grid = branches[0](images, all_screens, pick, order, places, taper)
+        grid = branches[0](images, all_screens, pick, order, places)
     else:
         index = sum((most[0, 0] > rows).astype(jnp.int32) for rows in heights[:-1])
-        grid = lax.switch(index, branches, images, all_screens, pick, order, places, taper)
+        grid = lax.switch(index, branches, images, all_screens, pick, order, places)
     return grid[None]
 
 

time: 107 us -> 104 us (0.972)
  Pallas kernels: 29.5 us -> 26.3 us
  waiting for transfers between devices: 10.6 us -> 9.26 us
    all_to_all x1, waiting for transfers between devices: 7.81 us -> 0.01 us  [per_device(): lax.all_to_all(every, ('corr', 'tile'), split_axis=0, concat_axis=0, tile...]
    ppermute x3, waiting for transfers between devices: 2.78 us -> 9.24 us  [per_device(): lax.ppermute(piece, 'corr', [(i, i ^ d) for i in range(groups)])]
    pallas_call x1, Pallas kernels: 12.6 us -> 10.9 us  [make_images(): pl.pallas_call(functools.partial(image_kernel, ncorr, groups), grid=(coun...]
    pallas_call x1, Pallas kernels: 9.87 us -> 8.33 us  [place_on_grid(): pl.pallas_call(functools.partial(grid_kernel, rows), in_specs=[pl.BlockSp...]
  transfers between devices with their start and end apart: 5 -> 5, of which waited for: 2 -> 2; matrix products, arithmetic and copies ran while one was open for 1% -> 2% of each run, Pallas kernels for 13% -> 12%
where the time goes in v1:
time: 104 us; the launch traced here: 103 us
  blocking collectives  37.9 us (36%)
  Pallas kernels  26.3 us (25%)
  between operations  14.8 us (14%)
  starting transfers between devices  10.8 us (10%)
  waiting for transfers between devices  9.26 us (9%)
  local copies, waits for them, and re-layouts  3.01 us (3%)
    all_to_all x1, blocking collectives, finish(): lax.all_to_all(sending.reshape(groups * owners, rows, 2 * local), ('corr'...  37.9 us
    pallas_call x1, Pallas kernels, make_images(): pl.pallas_call(functools.partial(image_kernel, ncorr, groups), grid=(coun...  10.9 us
    ppermute x3, waiting for transfers between devices, per_device(): lax.ppermute(piece, 'corr', [(i, i ^ d) for i in range(groups)])  9.24 us
    pallas_call x1, Pallas kernels, place_on_grid(): pl.pallas_call(functools.partial(grid_kernel, rows), in_specs=[pl.BlockSp...  8.33 us
    all_to_all x1, starting transfers between devices, per_device(): lax.all_to_all(every, ('corr', 'tile'), split_axis=0, concat_axis=0, tile...  7.3 us
    pallas_call x1, Pallas kernels, apply_aterms(): pl.pallas_call(functools.partial(aterm_kernel, ncorr, owners, rows, scale...  5.96 us
    ppermute x3, starting transfers between devices, per_device(): lax.ppermute(piece, 'corr', [(i, i ^ d) for i in range(groups)])  3.49 us
  transfers between devices with their start and end apart: 5, of which 2 were waited for; matrix products, arithmetic and copies ran while one was open for 2% of the time, Pallas kernels for 12%

profile of v1, /device:TPU:0, one launch (start us, length us, event | category | flops | bytes accessed | tf_op | source)
XLA Modules:
  0.0 102.7 jit_solution(469103828345317848)
XLA Ops:
  6.5 0.0 all-gather.2.cloned.1.call-start
  6.5 1.0 constant_dynamic-slice_fusion
  7.5 0.8 copy.20
  8.3 0.0 all-gather.2.cloned.1.call-update
  8.3 0.7 pad_add_fusion
  9.0 0.7 broadcast_in_dim.16
  9.7 7.3 %all-to-all-start.3 = ((s32[32,8,128]{2,1,0:T(8,128)}), s32[32,8,128]{2,1,0:T(8,128)S(1)}, u32[]{:S(2)}, u32[]{:S(2)}) async-start(s32[32,8,128]{2,1,0:T(8,128)} %broadcast_in_dim.16), calls=%async_computation.3 | async-start | bytes 262144 | tf_op jit(solution)/shard_map/all_to_all | solution.py:426
  17.0 10.9 %images.1 = (bf16[64,2048]{1,0:T(8,128)(2,1)}, bf16[64,2048]{1,0:T(8,128)(2,1)}, bf16[64,2048]{1,0:T(8,128)(2,1)}, bf16[64,2048]{1,0:T(8,128)(2,1)}) custom-call(bf16[64,8,256]{2,1,0:T(8,128)(2,1)} %vis_ref.1, f32[3,64,256]{2,1,0:T(8,128)} %bitcast.33), custom_call_target="tpu_custom_call" | custom-call | flops 8589934592 | bytes 2097152 | tf_op jit(solution)/shard_map/images/pallas_call | solution.py:116
  27.9 1.8 %collective-permute-start = (bf16[64,2048]{1,0:T(8,128)(2,1)}, bf16[64,2048]{1,0:T(8,128)(2,1)S(1)}, u32[]{:S(2)}, u32[]{:S(2)}) collective-permute-start(bf16[64,2048]{1,0:T(8,128)(2,1)} %get-tuple-element.110), channel_id=1, source_target_pairs={{0,8},{8,0},{16,24},{24,16},{1,9},{9,1},{17,25},{25,17},{2,10},{10... | collective-permute-start | bytes 786440 | tf_op jit(solution)/shard_map/ppermute | solution.py:430
  29.7 1.5 %collective-permute-start.1 = (bf16[64,2048]{1,0:T(8,128)(2,1)}, bf16[64,2048]{1,0:T(8,128)(2,1)}, u32[]{:S(2)}, u32[]{:S(2)}) collective-permute-start(bf16[64,2048]{1,0:T(8,128)(2,1)} %get-tuple-element.111), channel_id=1, source_target_pairs={{0,16},{8,24},{16,0},{24,8},{1,17},{9,25},{17,1},{25,9},{2,18},{10... | collective-permute-start | bytes 786440 | tf_op jit(solution)/shard_map/ppermute | solution.py:430
  31.2 0.2 collective-permute-start.2
  31.4 0.0 all-to-all-done.3.every_ref
  31.4 1.1 %plan.1 = (bf16[512,512]{1,0:T(8,128)(2,1)}, f32[8,256]{1,0:T(8,128)S(1)}, s32[8,8,128]{2,1,0:T(8,128)S(1)}, s32[8,128]{1,0:T(8,128)S(1)}) custom-call(s32[32,8,128]{2,1,0:T(8,128)S(1)} %all-to-all-done.3.every_ref), custom_call_target="tpu_custom_call" | custom-call | flops 1073741824 | bytes 1048576 | tf_op jit(solution)/shard_map/plan/pallas_call | solution.py:189
  32.5 0.6 slice.4
  34.5 2.8 %collective-permute-done = bf16[64,2048]{1,0:T(8,128)(2,1)S(1)} collective-permute-done((bf16[64,2048]{1,0:T(8,128)(2,1)}, bf16[64,2048]{1,0:T(8,128)(2,1)S(1)}, u32[]{:S(2)}, u32[]{:S(2)}) %collective-permute-start) | collective-permute-done | bytes 262176 | tf_op jit(solution)/shard_map/ppermute | solution.py:430
  37.2 6.5 %collective-permute-done.1 = bf16[64,2048]{1,0:T(8,128)(2,1)} collective-permute-done((bf16[64,2048]{1,0:T(8,128)(2,1)}, bf16[64,2048]{1,0:T(8,128)(2,1)}, u32[]{:S(2)}, u32[]{:S(2)}) %collective-permute-start.1) | collective-permute-done | bytes 262176 | tf_op jit(solution)/shard_map/ppermute | solution.py:430
  43.7 0.0 collective-permute-done.2
  43.7 0.0 all-gather.2.cloned.1.call-done
  43.7 52.2 %conditional.1 = (f32[1,8,2,128,128]{4,3,2,1,0:T(8,128)}) conditional(s32[]{:T(128)} %bitcast.12, (bf16[64,2048]{1,0:T(8,128)(2,1)}, bf16[64,2048]{1,0:T(8,128)(2,1)S(1)}, bf16[64,2048]{1,0:T(8,128)(2,1)}, bf16[64,2048]{1,0:T(8,128)(2,1)}, bf16[512,2048]{1,0:T(8,128)(2,1)}, /*index=5*/bf16[512,512]{1,0:T(8,128)(2,1)}, ...), branch_computations={%region_0.1_spmd, %region_1.2_spmd, %region_2.3_spmd} | conditional | flops 6442450944 | bytes 16777280 | solution.py:449
  43.7 6.0 %aterms.3 = bf16[4,320,512]{2,1,0:T(8,128)(2,1)} custom-call(bf16[64,2048]{1,0:T(8,128)(2,1)} %get-tuple-element.71.refs_0_, bf16[64,2048]{1,0:T(8,128)(2,1)S(1)} %get-tuple-element.72.refs_1_, bf16[64,2048]{1,0:T(8,128)(2,1)} %get-tuple-element.73.refs_2_, bf16[64,2048]{1,0:T(8,128)(2,1)} %get-tuple-element.74.refs_3_, ...), custom_call_target="tpu_custom_call" | custom-call | flops 6442450944 | bytes 8388608 | tf_op jit(solution)/shard_map/cond/branch_0_fun/aterms/pallas_call | solution.py:271
  49.7 37.9 %all_to_all.17 = bf16[32,40,512]{2,1,0:T(8,128)(2,1)S(1)} all-to-all(bf16[32,40,512]{2,1,0:T(8,128)(2,1)} %bitcast.27), channel_id=1, replica_groups=mesh['corr'=4,'tile'=8] {'corr','tile'}, dimensions={0} | all-to-all | bytes 2621440 | tf_op jit(solution)/shard_map/cond/branch_0_fun/all_to_all | solution.py:438
  87.5 0.0 copy-done.2
  87.5 0.0 copy-done.3
  87.5 8.3 %grid.3 = f32[8,2,128,128]{3,2,1,0:T(8,128)} custom-call(s32[8,8,128]{2,1,0:T(8,128)S(1)} %get-tuple-element.70.place_ref, bf16[4,320,512]{2,1,0:T(8,128)(2,1)S(1)} %bitcast.24, bf16[512,512]{1,0:T(8,128)(2,1)S(1)} %copy-done.3, bf16[512,512]{1,0:T(8,128)(2,1)S(1)} %copy-done.2), custom_call_target="tpu_custom_call" | custom-call | tf_op jit(solution)/shard_map/cond/branch_0_fun/grid/pallas_call | solution.py:358
  (3 shorter events, 0.0 us)
Async XLA Ops:
  6.5 37.2 %all-gather.2.cloned.1.call-start = ((), (), s32[]{:S(2)}) async-start(), calls=%async_computation.4 | async-start | bytes 2359296 | tf_op jit(solution)/shard_map/all_gather | solution.py:421
  9.7 21.7 %all-to-all-start.3 = ((s32[32,8,128]{2,1,0:T(8,128)}), s32[32,8,128]{2,1,0:T(8,128)S(1)}, u32[]{:S(2)}, u32[]{:S(2)}) async-start(s32[32,8,128]{2,1,0:T(8,128)} %broadcast_in_dim.16), calls=%async_computation.3 | async-start | bytes 262144 | tf_op jit(solution)/shard_map/all_to_all | solution.py:426
  27.9 9.3 %collective-permute-start = (bf16[64,2048]{1,0:T(8,128)(2,1)}, bf16[64,2048]{1,0:T(8,128)(2,1)S(1)}, u32[]{:S(2)}, u32[]{:S(2)}) collective-permute-start(bf16[64,2048]{1,0:T(8,128)(2,1)} %get-tuple-element.110), channel_id=1, source_target_pairs={{0,8},{8,0},{16,24},{24,16},{1,9},{9,1},{17,25},{25,17},{2,10},{10... | collective-permute-start | bytes 786440 | tf_op jit(solution)/shard_map/ppermute | solution.py:430
  29.7 14.0 %collective-permute-start.1 = (bf16[64,2048]{1,0:T(8,128)(2,1)}, bf16[64,2048]{1,0:T(8,128)(2,1)}, u32[]{:S(2)}, u32[]{:S(2)}) collective-permute-start(bf16[64,2048]{1,0:T(8,128)(2,1)} %get-tuple-element.111), channel_id=1, source_target_pairs={{0,16},{8,24},{16,0},{24,8},{1,17},{9,25},{17,1},{25,9},{2,18},{10... | collective-permute-start | bytes 786440 | tf_op jit(solution)/shard_map/ppermute | solution.py:430
  31.2 12.6 %collective-permute-start.2 = (bf16[64,2048]{1,0:T(8,128)(2,1)}, bf16[64,2048]{1,0:T(8,128)(2,1)}, u32[]{:S(2)}, u32[]{:S(2)}) collective-permute-start(bf16[64,2048]{1,0:T(8,128)(2,1)} %get-tuple-element.112), channel_id=1, source_target_pairs={{0,24},{8,16},{16,8},{24,0},{1,25},{9,17},{17,9},{25,1},{2,26},{10... | collective-permute-start | bytes 786440 | tf_op jit(solution)/shard_map/ppermute | solution.py:430
  49.7 37.9 %copy-start.2 = (bf16[512,512]{1,0:T(8,128)(2,1)S(1)}, bf16[512,512]{1,0:T(8,128)(2,1)}, u32[]{:S(2)}) copy-start(bf16[512,512]{1,0:T(8,128)(2,1)} %constant.27.clone.1.row_ref) | copy-start | bytes 1572868 | tf_op jit(solution)/shard_map/cond
  49.7 37.9 %copy-start.3 = (bf16[512,512]{1,0:T(8,128)(2,1)S(1)}, bf16[512,512]{1,0:T(8,128)(2,1)}, u32[]{:S(2)}) copy-start(bf16[512,512]{1,0:T(8,128)(2,1)} %constant.26.clone.1.col_ref) | copy-start | bytes 1572868 | tf_op jit(solution)/shard_map/cond
Sparse Core Ops, SparseCore 0:
  9.0 32.9 all-gather.1
